TPU v7x, 32 devices: a whole 2x2x4 slice. The times are simulated.
32 devices in a mesh: seq: 16 (over z, y, x), trk: 2 (over core).
Axes of the slice: x: 2, y: 2, z: 4, core: 2. Of those that a mesh axis runs over, the one named last changes fastest.
Arguments:
- embeddings: bfloat16 [4, 2048, 1920], P(None, 'seq', 'trk'), may hold values from -6 to 6
- head: bfloat16 [1920, 4096], P(None, 'trk'), may hold values from -0.125 to 0.125
- exon_starts: int32 [4, 32, 8], replicated, may hold values from 0 to 2040, as said below
- exon_lengths: int32 [4, 32, 8], replicated, may hold values from 1 to 8, as said below
- gene_owner: int32 [4, 32], replicated, may hold values from 0 to 15, as said below
- gene_targets: float32 [4, 64, 4096], P(None, 'seq', 'trk'), may hold values from 2 to 400, as said below
Outputs:
- gene_pred: float32 [4, 64, 4096], P(None, 'seq', 'trk')
- loss: float32 [4, 4096], P(None, 'trk')
- grad_head: float32 [1920, 4096], P('seq', 'trk')
Inputs may be any that keep to these rules, and one draw needn't show every extreme that they name: `exon_starts`: each gene has 8 exon blocks; blocks may intersect. Some block of each window starts at 0 and some at 2040. `exon_lengths`: some block of each window has length 8. `gene_owner`: in each window no owner holds more than 4 genes, and some owner holds exactly 4. `gene_targets`: entries of empty slots are read by nothing.
All inputs are finite; a program needn't handle non-finite values.
Results may differ from a plain program's by a relative error of at most 0.0041.
Values may be sent and summed in bfloat16 or wider, within the bound.
A program may use at most 128 MiB of HBM per device.

v0:
```python
import jax
import jax.numpy as jnp
from jax import lax
from jax.sharding import PartitionSpec as P


def slot_table(gene_owner, capacity):
    genes = gene_owner.shape[1]
    same = gene_owner[:, :, None] == gene_owner[:, None, :]
    earlier = jnp.arange(genes)[None, :] < jnp.arange(genes)[:, None]
    ahead = jnp.sum((same & earlier[None]).astype(jnp.int32), axis=2)
    return gene_owner * capacity + ahead


def coverage(starts, lengths, positions):
    where_bin = positions[None, None, None, :]
    inside = (where_bin >= starts[..., None]) & (where_bin < (starts + lengths)[..., None])
    return jnp.sum(inside.astype(jnp.float32), axis=2)


def fold_sources(received):
    return jnp.sum(received, axis=1)


def per_device(embeddings, head, exon_starts, exon_lengths, gene_owner, gene_targets):
    seq_devices = lax.axis_size("seq")
    seq_place = lax.axis_index("seq")
    windows, bin_dev, _ = embeddings.shape
    genes = gene_owner.shape[1]
    capacity = gene_targets.shape[1]
    slot_total = seq_devices * capacity
    whole = lax.all_gather(embeddings, "trk", axis=2, tiled=True)
    logits = jnp.einsum("wbd,dt->wbt", whole, head, preferred_element_type=jnp.float32)
    pred = jax.nn.softplus(logits).astype(jnp.bfloat16)
    positions = seq_place * bin_dev + jnp.arange(bin_dev, dtype=jnp.int32)
    cover = coverage(exon_starts, exon_lengths, positions)
    slot_of = slot_table(gene_owner, capacity)
    onehot = (slot_of[..., None] == jnp.arange(slot_total, dtype=jnp.int32)).astype(jnp.float32)
    member = jnp.einsum("wgs,wgb->wsb", onehot, cover, precision=lax.Precision.HIGHEST).astype(
        jnp.bfloat16
    )
    valid = jnp.sum(onehot, axis=1)
    valid_here = lax.dynamic_slice_in_dim(valid, seq_place * capacity, capacity, 1)
    targets_here = gene_targets * valid_here[..., None]
    target_part = jnp.sum(targets_here, axis=1)
    partial_value = jnp.einsum("wsb,wbt->wst", member, pred, preferred_element_type=jnp.float32)
    total, target_sum = lax.psum((jnp.sum(partial_value, axis=1), target_part), "seq")
    blocks = partial_value.reshape(windows, seq_devices, capacity, partial_value.shape[2])
    gene_here = fold_sources(lax.all_to_all(blocks, "seq", split_axis=1, concat_axis=1, tiled=True))
    safe = jnp.where(valid_here[..., None] > 0, gene_here, 1.0)
    fit_part = jnp.sum(targets_here * jnp.log(safe), axis=1)
    scale_rows = (genes / target_sum)[:, None, :]
    gene_grad = (
        scale_rows
        * (
            valid_here[..., None] * (0.2 + 0.8 * target_sum / total)[:, None, :]
            - targets_here / safe
        )
    ).astype(jnp.bfloat16)
    bin_grad = jnp.einsum(
        "wsb,wst->wbt",
        member,
        lax.all_gather(gene_grad, "seq", axis=1, tiled=True),
        preferred_element_type=jnp.float32,
    )
    logit_grad = (bin_grad * jax.nn.sigmoid(logits)).astype(jnp.bfloat16)
    grad_head = lax.psum_scatter(
        jnp.einsum("wbd,wbt->dt", whole, logit_grad, preferred_element_type=jnp.float32),
        "seq",
        scatter_dimension=0,
        tiled=True,
    )
    fit = lax.psum(fit_part, "seq")
    log_total = jnp.log(total)
    loss = (-fit + target_sum * log_total + 0.2 * (total - target_sum * log_total)) / target_sum
    return (gene_here, loss, grad_head)


def solution(mesh):
    return jax.shard_map(
        per_device,
        mesh=mesh,
        in_specs=(P(None, "seq", "trk"), P(None, "trk"), P(), P(), P(), P(None, "seq", "trk")),
        out_specs=(P(None, "seq", "trk"), P(None, "trk"), P("seq", "trk")),
        check_vma=False,
    )
```

profile of v0, /device:TPU:14, one launch (start us, length us, event | category | flops | bytes accessed | tf_op | source)
XLA Modules:
  0.0 528.4 jit_solution(8892406837950601786)
XLA Ops:
  7.2 0.7 all-gather.3.cloned.1.call-update
  7.9 0.8 copy.27
  8.7 0.7 add.46
  9.5 1.0 convert_reduce_fusion.2
  10.5 0.4 convert_reduce_fusion
  10.9 0.7 multiply_add_fusion
  11.6 0.4 convolution_convert_fusion
  11.9 9.4 %all-gather.3.cloned.1.call-done = bf16[4,128,1920]{1,2,0:T(8,128)(2,1)} async-done(((bf16[4,128,960]{1,2,0:T(8,128)(2,1)}), bf16[4,128,1920]{1,2,0:T(8,128)(2,1)}) %all-gather.3.cloned.1.call-update) | async-done | bytes 1966096 | tf_op jit(solution)/shard_map/all_gather | solution.py:32
  21.3 7.7 %fusion.4 = (u8[128,2048]{1,0:T(8,128)(4,1)S(1)}, f32[4,128,2048]{2,1,0:T(8,128)S(1)}) fusion(bf16[4,128,1920]{1,2,0:T(8,128)(2,1)} %all-gather.3.cloned.1.call-done, bf16[1920,2048]{1,0:T(8,128)(2,1)} %param.7), kind=kOutput, calls=%fused_computation.10 | convolution fusion | flops 4031512576 | bytes 14286848 | tf_op jit(solution)/shard_map/wbd,dt->wbt/dot_general | solution.py:33
  29.0 4.8 fusion.13
  33.8 1.9 reshape.35
  35.7 1.5 copy.29
  37.2 7.1 %all-to-all-start = ((f32[4,16,4,2048]{3,2,0,1:T(4,128)}), f32[4,16,4,2048]{3,2,0,1:T(4,128)S(1)}, u32[]{:S(2)}, u32[]{:S(2)}) async-start(f32[4,16,4,2048]{3,2,0,1:T(4,128)} %copy.29), calls=%async_computation | async-start | bytes 4194304 | tf_op jit(solution)/shard_map/all_to_all | solution.py:49
  44.5 48.3 %all-to-all-done = f32[4,16,4,2048]{3,2,0,1:T(4,128)S(1)} async-done(((f32[4,16,4,2048]{3,2,0,1:T(4,128)}), f32[4,16,4,2048]{3,2,0,1:T(4,128)S(1)}, u32[]{:S(2)}, u32[]{:S(2)}) %all-to-all-start) | async-done | bytes 2097184 | tf_op jit(solution)/shard_map/all_to_all | solution.py:49
  92.7 0.5 reduce_sum.65
  93.3 0.9 multiply_reduce_fusion
  94.2 104.1 %all-reduce.3.cloned.1.call-done = (f32[4,2048]{1,0:T(4,128)}, f32[4,2048]{1,0:T(4,128)}, f32[4,2048]{1,0:T(4,128)}) async-done(((f32[4,2048]{1,0:T(4,128)}, f32[4,2048]{1,0:T(4,128)}, f32[4,2048]{1,0:T(4,128)}), (f32[4,2048]{1,0:T(4,128)}, f32[4,2048]{1,0:T(4,128)}, f32[4,2048]{1,0:T(4,128)})) %all-reduce.3.cloned.1.call-update) | async-done | bytes 98320 | tf_op jit(solution)/shard_map/psum | solution.py:47
  198.4 1.4 fusion.9
  199.8 0.2 multiply_convert_fusion.1
  200.0 0.7 copy.30
  200.7 54.5 %all-gather.5.cloned.1.call-done = bf16[4,64,2048]{2,0,1:T(4,128)(2,1)} async-done(((bf16[4,4,2048]{2,0,1:T(4,128)(2,1)}), bf16[4,64,2048]{2,0,1:T(4,128)(2,1)}) %all-gather.5.cloned.1.call-update) | async-done | bytes 1048592 | tf_op jit(solution)/shard_map/all_gather | solution.py:63
  255.2 11.7 %convolution_bitcast_fusion = f32[1920,2048]{0,1:T(8,128)} fusion(bf16[4,128,1920]{1,2,0:T(8,128)(2,1)} %all-gather.3.cloned.1.call-done, f32[4,128,2048]{2,1,0:T(8,128)} %copy-done.2, bf16[4,64,128]{2,1,0:T(8,128)(2,1)S(1)} %convolution_convert_fusion, bf16[4,64,2048]{2,0,1:T(4,128)(2,1)} %all-gather.5.cloned.1.call-done), kind=kOutput, calls=%fused_computation | convolution fusion | flops 4165992448 | bytes 23003136 | tf_op jit(solution)/shard_map/wbd,wbt->dt/dot_general | solution.py:68
  266.9 15.7 %copy.35 = f32[1920,2048]{1,0:T(8,128)} copy(f32[1920,2048]{0,1:T(8,128)} %convolution_bitcast_fusion) | data formatting | bytes 31457280
  282.7 239.2 %reduce-scatter.4.cloned.1.call-done = f32[120,2048]{1,0:T(8,128)} async-done(((f32[1920,2048]{1,0:T(8,128)}), f32[120,2048]{1,0:T(8,128)}) %reduce-scatter.4.cloned.1.call-update) | async-done | bytes 983056
  (18 shorter events, 0.5 us)
Async XLA Ops:
  7.2 14.1 %all-gather.3.cloned.1.call-start = ((), (), s32[]{:S(2)}) async-start(), calls=%async_computation.2 | async-start | bytes 2949120 | tf_op jit(solution)/shard_map/all_gather | solution.py:32
  29.0 4.8 copy-start.2
  37.2 56.1 %copy-start.1 = (f32[4,4,2048]{2,1,0:T(4,128)S(1)}, f32[4,4,2048]{2,1,0:T(4,128)}, u32[]{:S(2)}) copy-start(f32[4,4,2048]{2,1,0:T(4,128)} %param.11) | copy-start | bytes 393220
  37.2 55.6 %all-to-all-start = ((f32[4,16,4,2048]{3,2,0,1:T(4,128)}), f32[4,16,4,2048]{3,2,0,1:T(4,128)S(1)}, u32[]{:S(2)}, u32[]{:S(2)}) async-start(f32[4,16,4,2048]{3,2,0,1:T(4,128)} %copy.29), calls=%async_computation | async-start | bytes 4194304 | tf_op jit(solution)/shard_map/all_to_all | solution.py:49
  44.2 154.1 %all-reduce.3.cloned.1.call-start = ((), (), s32[]{:S(2)}) async-start(), calls=%async_computation.5 | async-start | bytes 196608 | tf_op jit(solution)/shard_map/psum | solution.py:47
  93.2 173.7 %copy-start = (f32[4,4,2048]{2,1,0:T(4,128)}, f32[4,4,2048]{2,1,0:T(4,128)S(1)}, u32[]{:S(2)}) copy-start(f32[4,4,2048]{2,1,0:T(4,128)S(1)} %reduce_sum.65) | copy-start | bytes 393220
  94.2 161.0 %all-gather.5.cloned.1.call-start = ((), (), s32[]{:S(2)}) async-start(), calls=%async_computation.3 | async-start | bytes 1114112 | tf_op jit(solution)/shard_map/all_gather | solution.py:63
  200.7 321.2 %reduce-scatter.4.cloned.1.call-start = ((), (), s32[]{:S(2)}) async-start(), calls=%async_computation.4 | async-start | bytes 16711680
Sparse Core Ops, SparseCore 0:
  9.5 11.7 all-gather.2
  94.3 104.0 all-reduce.2
  201.7 53.4 all-gather.4
  282.8 238.9 reduce-scatter.3
where the time goes:
time: 531 us; the launch traced here: 528 us
  waiting for transfers between devices  456 us (86%)
  matrix products  24.5 us (5%)
  local copies, waits for them, and re-layouts  20.6 us (4%)
  between operations  13.9 us (3%)
  starting transfers between devices  7.25 us (1%)
  other arithmetic  5.93 us (1%)
    unnamed x5, waiting for transfers between devices  240 us
    psum x1, waiting for transfers between devices, per_device(): lax.psum((jnp.sum(partial_value, axis=1), target_part), 'seq')  104 us
    all_gather x1, waiting for transfers between devices, per_device(): lax.all_gather(gene_grad, 'seq', axis=1, tiled=True)  54.5 us
    all_to_all x1, waiting for transfers between devices, per_device(): lax.all_to_all(blocks, 'seq', split_axis=1, concat_axis=1, tiled=True)  48.3 us
    unnamed x8, local copies, waits for them, and re-layouts  16.5 us
    dot_general x1, matrix products, per_device(): jnp.einsum('wbd,wbt->dt', whole, logit_grad, preferred_element_type=jnp.f...  11.7 us
  transfers between devices with their start and end apart: 5, of which 5 were waited for; matrix products, arithmetic and copies ran while one was open for 1% of the time, Pallas kernels for 0%

commit v1 on v0

v1 whole, which is shorter than its diff:
```python
import functools

import jax
import jax.numpy as jnp
from jax import lax
from jax.experimental import pallas as pl
from jax.experimental.pallas import tpu as pltpu
from jax.sharding import PartitionSpec as P

MESH = pl.DeviceIdType.MESH
HIGHEST = lax.Precision.HIGHEST


def slot_table(gene_owner, capacity):
    genes = gene_owner.shape[1]
    same = gene_owner[:, :, None] == gene_owner[:, None, :]
    earlier = jnp.arange(genes)[None, :] < jnp.arange(genes)[:, None]
    ahead = jnp.sum((same & earlier[None]).astype(jnp.int32), axis=2)
    return gene_owner * capacity + ahead


def coverage(starts, lengths, positions):
    where_bin = positions[None, None, None, :]
    inside = (where_bin >= starts[..., None]) & (where_bin < (starts + lengths)[..., None])
    return jnp.sum(inside.astype(jnp.float32), axis=2)


def kernel(
    dims,
    x_ref, head_ref, mem_ref, pick_ref, give_ref, tgt_ref,
    grad_ref, gene_ref, loss_ref,
    x_all, pred, sig, part, part_in, grads, tgt_in, gene_out, loss_out, lgrad, acc, block_out, block_in,
    near_send, near_recv, sib_send, sib_recv, tgt_send, tgt_recv, part_send, part_recv,
    grads_send, grads_recv, gene_send, gene_recv, loss_send, loss_recv, block_send, block_recv,
):
    n_seq, n_trk, windows, group, genes, own_rows = dims
    me = lax.axis_index("seq")
    core = lax.axis_index("trk")
    win = me // group
    place = lax.rem(me, group)
    rows = x_ref.shape[0]
    chans = x_ref.shape[1]
    tracks = head_ref.shape[2]
    tile = 256 if rows % 256 == 0 else rows

    def to_seq(src, dst, send, recv, there):
        return pltpu.make_async_remote_copy(
            src_ref=src, dst_ref=dst, send_sem=send, recv_sem=recv,
            device_id={"seq": there}, device_id_type=MESH,
        )

    def to_core(src, dst, send, recv, there):
        return pltpu.make_async_remote_copy(
            src_ref=src, dst_ref=dst, send_sem=send, recv_sem=recv,
            device_id={"trk": there}, device_id_type=MESH,
        )

    barrier = pltpu.get_barrier_semaphore()

    @pl.loop(1, n_seq)
    def _(k):
        pl.semaphore_signal(
            barrier, inc=1, device_id={"seq": lax.rem(me + k, n_seq)}, device_id_type=MESH
        )

    for k in range(1, n_trk):
        pl.semaphore_signal(
            barrier, inc=1, device_id={"trk": lax.rem(core + k, n_trk)}, device_id_type=MESH
        )
    pl.semaphore_wait(barrier, n_seq - 1 + n_trk - 1)

    def near(k):
        there = lax.rem(place + k, group)
        return to_seq(
            x_ref, x_all.at[core, place], near_send.at[there], near_recv.at[place],
            win * group + there,
        )

    def near_arrival(k):
        frm = lax.rem(place + k, group)
        return to_seq(
            x_ref, x_all.at[core, frm], near_send.at[frm], near_recv.at[frm], win * group + frm
        )

    def sibling(k, source, slot):
        there = lax.rem(core + k, n_trk)
        return to_core(
            source, x_all.at[core, slot], sib_send.at[there, slot], sib_recv.at[core, slot], there
        )

    def sibling_arrival(k, slot):
        frm = lax.rem(core + k, n_trk)
        return to_core(
            x_ref, x_all.at[frm, slot], sib_send.at[frm, slot], sib_recv.at[frm, slot], frm
        )

    for k in range(1, group):
        near(k).start()
    for k in range(1, n_trk):
        sibling(k, x_ref, place).start()
    x_all[core, place] = x_ref[...]

    def tgt_copy(k):
        there = lax.rem(me + k, n_seq)
        return to_seq(tgt_ref.at[there], tgt_in.at[me], tgt_send.at[there], tgt_recv.at[me], there)

    @pl.loop(1, n_seq)
    def _(k):
        tgt_copy(k).start()

    tgt_in[me] = tgt_ref[me]

    part[...] = jnp.zeros_like(part)

    def forward(slot):
        @pl.loop(0, rows // tile)
        def _(i):
            at = pl.ds(pl.multiple_of(i * tile, tile), tile)
            logits = jnp.dot(
                x_all[0, slot, at, :], head_ref[0], preferred_element_type=jnp.float32
            )
            for c in range(1, n_trk):
                logits += jnp.dot(
                    x_all[c, slot, at, :], head_ref[c], preferred_element_type=jnp.float32
                )
            small = jnp.exp(-jnp.abs(logits))
            pred[at, :] = (jnp.maximum(logits, 0.0) + jnp.log1p(small)).astype(jnp.bfloat16)
            sig[slot, at, :] = jnp.where(logits >= 0, 1.0, small) / (1.0 + small)

        part[...] += jnp.dot(
            mem_ref[slot], pred[...], preferred_element_type=jnp.float32
        ).reshape(part.shape)

    for k in range(1, group + 1):
        if k < group:
            near_arrival(k).wait_recv()
            frm = lax.rem(place + k, group)
            for j in range(1, n_trk):
                sibling(j, x_all.at[core, frm], frm).start()
        slot = lax.rem(place + k - 1, group)
        for j in range(1, n_trk):
            sibling_arrival(j, slot).wait_recv()
        forward(slot)

    def part_copy(k):
        there = lax.rem(win + k, windows)
        return to_seq(
            part.at[there], part_in.at[win], part_send.at[there], part_recv.at[win],
            there * group + place,
        )

    for k in range(1, windows):
        part_copy(k).start()

    @pl.loop(1, n_seq)
    def _(k):
        frm = lax.rem(me + k, n_seq)
        to_seq(
            tgt_ref.at[frm], tgt_in.at[frm], tgt_send.at[frm], tgt_recv.at[frm], frm
        ).wait_recv()

    tgt = jnp.dot(
        pick_ref[...], tgt_in[...].reshape(-1, tracks),
        preferred_element_type=jnp.float32, precision=HIGHEST,
    )
    tsum = jnp.sum(tgt, axis=0, keepdims=True)
    part_in[win] = part[win]
    for k in range(1, windows):
        frm = lax.rem(win + k, windows)
        to_seq(
            part.at[frm], part_in.at[frm], part_send.at[frm], part_recv.at[frm],
            frm * group + place,
        ).wait_recv()
    gene = part_in[0]
    for k in range(1, windows):
        gene += part_in[k]
    total = jnp.sum(gene, axis=0, keepdims=True)
    grads[win] = (
        (genes / tsum) * ((0.2 + 0.8 * tsum / total) - tgt / gene)
    ).astype(jnp.bfloat16)

    def grads_copy(k):
        there = lax.rem(win + k, windows)
        return to_seq(
            grads.at[win], grads.at[win], grads_send.at[there], grads_recv.at[win],
            there * group + place,
        )

    for k in range(1, windows):
        grads_copy(k).start()

    fit = jnp.sum(tgt * jnp.log(gene), axis=0, keepdims=True)
    log_total = jnp.log(total)
    loss = (-fit + tsum * log_total + 0.2 * (total - tsum * log_total)) / tsum
    loss_out[...] = jnp.broadcast_to(loss, loss_out.shape)
    gene_out[...] = jnp.dot(
        give_ref[...], gene, preferred_element_type=jnp.float32, precision=HIGHEST
    ).reshape(gene_out.shape)

    def gene_copy(k):
        there = lax.rem(me + k, n_seq)
        return to_seq(
            gene_out.at[there], gene_ref.at[me], gene_send.at[there], gene_recv.at[me], there
        )

    def loss_copy(k):
        there = lax.rem(me + k, n_seq)
        return to_seq(loss_out, loss_ref.at[me], loss_send.at[there], loss_recv.at[me], there)

    gene_ref[me] = gene_out[me]
    loss_ref[me] = loss_out[...]

    for k in range(1, windows):
        frm = lax.rem(win + k, windows)
        to_seq(
            grads.at[frm], grads.at[frm], grads_send.at[frm], grads_recv.at[frm],
            frm * group + place,
        ).wait_recv()

    @pl.loop(1, n_seq)
    def _(k):
        gene_copy(k).start()
        loss_copy(k).start()

    @pl.loop(0, group)
    def _(slot):
        spread = lax.dot_general(
            mem_ref[slot], grads[...].reshape(-1, tracks), (((0,), (0,)), ((), ())),
            preferred_element_type=jnp.float32,
        )
        lgrad[slot] = (spread * sig[slot]).astype(jnp.bfloat16)

    blocks = n_seq // n_trk

    def block_copy(there):
        return to_seq(
            block_out.at[there], block_in.at[me], block_send.at[there], block_recv.at[me], there
        )

    for c in range(n_trk):
        acc[...] = jnp.zeros_like(acc)

        @pl.loop(0, group)
        def _(slot):
            acc[...] += lax.dot_general(
                x_all[c, slot], lgrad[slot], (((0,), (0,)), ((), ())),
                preferred_element_type=jnp.float32,
            )

        for j in range(blocks):
            there = c * blocks + j
            value = acc[j * own_rows:(j + 1) * own_rows].astype(jnp.bfloat16)
            spare = block_out.shape[1] - own_rows
            if spare:
                value = jnp.concatenate([value, jnp.zeros((spare, tracks), jnp.bfloat16)], axis=0)
            block_out[there] = value

            @pl.when(me != there)
            def _():
                block_copy(there).start()

    block_in[me] = block_out[me]

    @pl.loop(1, n_seq)
    def _(k):
        frm = lax.rem(me + k, n_seq)
        to_seq(
            block_out.at[frm], block_in.at[frm], block_send.at[frm], block_recv.at[frm], frm
        ).wait_recv()

    for p in range(group):
        whole = block_in[p].astype(jnp.float32)
        for w in range(1, windows):
            whole += block_in[w * group + p].astype(jnp.float32)
        grad_ref[p] = whole

    @pl.loop(1, n_seq)
    def _(k):
        frm = lax.rem(me + k, n_seq)
        to_seq(
            gene_out.at[frm], gene_ref.at[frm], gene_send.at[frm], gene_recv.at[frm], frm
        ).wait_recv()
        to_seq(loss_out, loss_ref.at[frm], loss_send.at[frm], loss_recv.at[frm], frm).wait_recv()
        tgt_copy(k).wait_send()
        gene_copy(k).wait_send()
        loss_copy(k).wait_send()
        block_copy(frm).wait_send()

    for k in range(1, windows):
        part_copy(k).wait_send()
        grads_copy(k).wait_send()
    for k in range(1, group):
        near(k).wait_send()
    for k in range(1, n_trk):
        sibling(k, x_ref, place).wait_send()
        for j in range(1, group):
            frm = lax.rem(place + j, group)
            sibling(k, x_all.at[core, frm], frm).wait_send()


def round_up(n, m):
    return (n + m - 1) // m * m


def per_device(embeddings, head, exon_starts, exon_lengths, gene_owner, gene_targets):
    n_seq = lax.axis_size("seq")
    n_trk = lax.axis_size("trk")
    me = lax.axis_index("seq")
    windows, bin_dev, chans = embeddings.shape
    genes = gene_owner.shape[1]
    capacity = gene_targets.shape[1]
    group = n_seq // windows
    win, place = me // group, me % group
    depth, track_dev = head.shape
    tracks = track_dev // group
    rows = windows * bin_dev
    own_rows = depth // n_seq
    row_pad = round_up(own_rows, 16)
    cap_pad = round_up(capacity, 8)
    bf16, f32 = jnp.bfloat16, jnp.float32

    positions = win * group * bin_dev + jnp.arange(group * bin_dev, dtype=jnp.int32)
    cover = coverage(exon_starts, exon_lengths, positions).reshape(windows, genes, group, bin_dev)
    same = jnp.eye(windows, dtype=f32)
    mem = cover.transpose(2, 0, 1, 3)[:, :, :, None, :] * same[None, :, None, :, None]
    mem = mem.reshape(group, windows * genes, rows).astype(bf16)
    slot_here = lax.dynamic_index_in_dim(slot_table(gene_owner, capacity), win, 0, keepdims=False)
    padded = slot_here // capacity * cap_pad + slot_here % capacity
    every = jnp.arange(n_seq * cap_pad, dtype=jnp.int32)
    pick = (padded[:, None] == every[None, :]).astype(f32)
    give = (padded[None, :] == every[:, None]).astype(f32)
    head_here = lax.dynamic_slice_in_dim(head, place * tracks, tracks, 1).reshape(
        n_trk, chans, tracks
    )
    tgt = gene_targets.reshape(windows, capacity, group, tracks).transpose(0, 2, 1, 3)
    tgt = jnp.pad(
        tgt.reshape(n_seq, capacity, tracks), ((0, 0), (0, cap_pad - capacity), (0, 0))
    )

    dma = pltpu.SemaphoreType.DMA
    vmem = pl.BlockSpec(memory_space=pltpu.VMEM)
    grad, gene, loss = pl.pallas_call(
        functools.partial(kernel, (n_seq, n_trk, windows, group, genes, own_rows)),
        out_shape=(
            jax.ShapeDtypeStruct((group, row_pad, tracks), f32),
            jax.ShapeDtypeStruct((n_seq, cap_pad, tracks), f32),
            jax.ShapeDtypeStruct((n_seq, 8, tracks), f32),
        ),
        in_specs=[vmem] * 6,
        out_specs=(vmem, vmem, vmem),
        scratch_shapes=[
            pltpu.VMEM((n_trk, group, rows, chans), bf16),
            pltpu.VMEM((rows, tracks), bf16),
            pltpu.VMEM((group, rows, tracks), f32),
            pltpu.VMEM((windows, genes, tracks), f32),
            pltpu.VMEM((windows, genes, tracks), f32),
            pltpu.VMEM((windows, genes, tracks), bf16),
            pltpu.VMEM((n_seq, cap_pad, tracks), f32),
            pltpu.VMEM((n_seq, cap_pad, tracks), f32),
            pltpu.VMEM((8, tracks), f32),
            pltpu.VMEM((group, rows, tracks), bf16),
            pltpu.VMEM((chans, tracks), f32),
            pltpu.VMEM((n_seq, row_pad, tracks), bf16),
            pltpu.VMEM((n_seq, row_pad, tracks), bf16),
            dma((group,)), dma((group,)),
            dma((n_trk, group)), dma((n_trk, group)),
            dma((n_seq,)), dma((n_seq,)),
            dma((windows,)), dma((windows,)),
            dma((windows,)), dma((windows,)),
            dma((n_seq,)), dma((n_seq,)),
            dma((n_seq,)), dma((n_seq,)),
            dma((n_seq,)), dma((n_seq,)),
        ],
        compiler_params=pltpu.CompilerParams(
            collective_id=0, has_side_effects=True, vmem_limit_bytes=60 * 1024 * 1024
        ),
    )(embeddings.reshape(rows, chans), head_here, mem, pick, give, tgt)

    grad_head = grad[:, :own_rows].transpose(1, 0, 2).reshape(own_rows, track_dev)
    gene_here = gene[:, :capacity].reshape(windows, group, capacity, tracks)
    gene_here = gene_here.transpose(0, 2, 1, 3).reshape(windows, capacity, track_dev)
    return gene_here, loss[:, 0].reshape(windows, track_dev), grad_head


def solution(mesh):
    return jax.shard_map(
        per_device,
        mesh=mesh,
        in_specs=(P(None, "seq", "trk"), P(None, "trk"), P(), P(), P(), P(None, "seq", "trk")),
        out_specs=(P(None, "seq", "trk"), P(None, "trk"), P("seq", "trk")),
        check_vma=False,
    )
```

time: 531 us -> 158 us (0.30)
  waiting for transfers between devices: 456 us -> 0 us
  Pallas kernels: 0 us -> 138 us
  matrix products: 24.5 us -> 0 us
  between operations: 13.9 us -> 0.79 us
  local copies, waits for them, and re-layouts: 20.6 us -> 13.1 us
  starting transfers between devices: 7.25 us -> 0 us
    unnamed x5 -> x0, waiting for transfers between devices: 240 us -> none
    pallas_call x0 -> x1, Pallas kernels: none -> 138 us  [per_device(): pl.pallas_call(functools.partial(kernel, (n_seq, n_trk, windows, group, g...]
    psum x1 -> x0, waiting for transfers between devices: 104 us -> none  [per_device(): lax.psum((jnp.sum(partial_value, axis=1), target_part), 'seq')]
    all_gather x2 -> x0, waiting for transfers between devices: 63.9 us -> none  [the longest x1 54.5 us: per_device(): lax.all_gather(gene_grad, 'seq', axis=1, tiled=True)]
    all_to_all x1 -> x0, waiting for transfers between devices: 48.3 us -> none  [per_device(): lax.all_to_all(blocks, 'seq', split_axis=1, concat_axis=1, tiled=True)]
    dot_general x4 -> x0, matrix products: 24.5 us -> none  [the longest x1 11.7 us: per_device(): jnp.einsum('wbd,wbt->dt', whole, logit_grad, preferred_element_type=jnp.f...]
    unnamed x8 -> x6, local copies, waits for them, and re-layouts: 16.5 us -> 3.38 us
    all_to_all x1 -> x0, starting transfers between devices: 7.09 us -> none  [per_device(): lax.all_to_all(blocks, 'seq', split_axis=1, concat_axis=1, tiled=True)]
  transfers between devices with their start and end apart: 5 -> 0, of which waited for: 5 -> 0; matrix products, arithmetic and copies ran while one was open for 1% -> 0% of each run, Pallas kernels for 0% -> 0%
where the time goes in v1:
time: 158 us
  Pallas kernels  138 us (87%)
  local copies, waits for them, and re-layouts  13.1 us (8%)
  other arithmetic  5.72 us (4%)
    pallas_call x1, Pallas kernels, per_device(): pl.pallas_call(functools.partial(kernel, (n_seq, n_trk, windows, group, g...  138 us
    unnamed x6, local copies, waits for them, and re-layouts  3.38 us

profile of v1, /device:TPU:14, one launch (start us, length us, event | category | flops | bytes accessed | tf_op | source)
XLA Modules:
  0.0 157.5 jit_solution(8572123601394232488)
XLA Ops:
  0.7 1.0 convert_reduce_fusion.1
  1.7 0.7 multiply_add_fusion
  2.4 0.7 fusion.1.pick_ref
  3.1 0.7 add.63
  3.8 0.1 copy.21
  3.9 0.6 fusion.give_ref
  4.5 0.8 copy.20
  5.3 0.9 convert_reduce_fusion
  6.3 0.1 reshape.112
  6.4 0.8 fusion.6
  7.3 0.7 pad.4.tgt_ref
  8.1 0.1 mul.52
  8.2 0.2 mul.50
  8.4 0.0 copy-start
  8.4 0.4 mul.51
  8.8 0.9 multiply_convert_fusion.mem_ref
  9.8 1.3 copy.19
  11.1 3.0 %constant_dynamic-slice_fusion.1 = bf16[1920,512]{1,0:T(8,128)(2,1)} fusion(bf16[1920,2048]{1,0:T(8,128)(2,1)} %param.7, s32[]{:T(128)S(6)} %select_n.44), kind=kLoop, calls=%fused_computation.31 | loop fusion | bytes 3932164 | tf_op jit(solution)/shard_map/dynamic_slice | solution.py:332
  14.0 137.9 %shard_map.85 = (f32[4,128,512]{2,1,0:T(8,128)}, f32[16,8,512]{2,1,0:T(8,128)}, f32[16,8,512]{2,1,0:T(8,128)}) custom-call(bf16[512,960]{1,0:T(8,128)(2,1)} %bitcast.33, bf16[2,960,512]{2,1,0:T(8,128)(2,1)} %bitcast.32, bf16[4,128,512]{2,1,0:T(8,128)(2,1)} %multiply_convert_fusion.mem_ref, f32[32,128]{1,0:T(8,128)} %fusion.1.pick_ref, ...), custom_call_target="tpu_custom_call" | custom-call | tf_op jit(solution)/shard_map/pallas_call | solution.py:342
  151.9 1.6 %slice.25 = f32[16,4,512]{2,1,0:T(4,128)} slice(f32[16,8,512]{2,1,0:T(8,128)} %get-tuple-element.6), slice={[0:16], [0:4], [0:512]} | slice | bytes 262144 | tf_op jit(solution)/shard_map/slice | solution.py:380
  153.5 1.0 slice_reduce_fusion
  154.6 0.6 reshape_squeeze.3
  155.2 1.3 slice_bitcast_fusion
  156.5 1.0 copy.25
  (10 shorter events, 0.2 us)
Async XLA Ops:
  8.4 1.4 copy-start

commit v2 on v1

--- a/solution.py
+++ b/solution.py
@@ -11,36 +11,26 @@
 HIGHEST = lax.Precision.HIGHEST
 
 
-def slot_table(gene_owner, capacity):
-    genes = gene_owner.shape[1]
-    same = gene_owner[:, :, None] == gene_owner[:, None, :]
-    earlier = jnp.arange(genes)[None, :] < jnp.arange(genes)[:, None]
-    ahead = jnp.sum((same & earlier[None]).astype(jnp.int32), axis=2)
-    return gene_owner * capacity + ahead
-
-
-def coverage(starts, lengths, positions):
-    where_bin = positions[None, None, None, :]
-    inside = (where_bin >= starts[..., None]) & (where_bin < (starts + lengths)[..., None])
-    return jnp.sum(inside.astype(jnp.float32), axis=2)
-
-
 def kernel(
     dims,
-    x_ref, head_ref, mem_ref, pick_ref, give_ref, tgt_ref,
+    x_hbm, head_hbm, starts_ref, lengths_ref, owner_ref, targets_ref,
     grad_ref, gene_ref, loss_ref,
-    x_all, pred, sig, part, part_in, grads, tgt_in, gene_out, loss_out, lgrad, acc, block_out, block_in,
+    x_all, head_ref, mem_ref, tgt_ref, gene_in, loss_in, pred, sig, part, part_in, grads, tgt_in, gene_out, loss_out, lgrad, acc, block_out, block_in,
     near_send, near_recv, sib_send, sib_recv, tgt_send, tgt_recv, part_send, part_recv,
     grads_send, grads_recv, gene_send, gene_recv, loss_send, loss_recv, block_send, block_recv,
+    diag_send, diag_recv, own_sem, head_sem,
 ):
     n_seq, n_trk, windows, group, genes, own_rows = dims
     me = lax.axis_index("seq")
     core = lax.axis_index("trk")
     win = me // group
     place = lax.rem(me, group)
-    rows = x_ref.shape[0]
-    chans = x_ref.shape[1]
+    rows, chans = x_all.shape[2:]
     tracks = head_ref.shape[2]
+    bin_dev = rows // windows
+    capacity = targets_ref.shape[1]
+    cap_pad = tgt_ref.shape[1]
+    square = group == 4 and rows % 32 == 0
     tile = 256 if rows % 256 == 0 else rows
 
     def to_seq(src, dst, send, recv, there):
@@ -69,17 +59,15 @@
         )
     pl.semaphore_wait(barrier, n_seq - 1 + n_trk - 1)
 
-    def near(k):
-        there = lax.rem(place + k, group)
-        return to_seq(
-            x_ref, x_all.at[core, place], near_send.at[there], near_recv.at[place],
+    def near_to(there):
+        return to_seq(
+            x_hbm, x_all.at[core, place], near_send.at[there], near_recv.at[place],
             win * group + there,
         )
 
-    def near_arrival(k):
-        frm = lax.rem(place + k, group)
-        return to_seq(
-            x_ref, x_all.at[core, frm], near_send.at[frm], near_recv.at[frm], win * group + frm
+    def near_from(frm):
+        return to_seq(
+            x_hbm, x_all.at[core, frm], near_send.at[frm], near_recv.at[frm], win * group + frm
         )
 
     def sibling(k, source, slot):
@@ -91,24 +79,92 @@
     def sibling_arrival(k, slot):
         frm = lax.rem(core + k, n_trk)
         return to_core(
-            x_ref, x_all.at[frm, slot], sib_send.at[frm, slot], sib_recv.at[frm, slot], frm
-        )
-
-    for k in range(1, group):
-        near(k).start()
+            x_hbm, x_all.at[frm, slot], sib_send.at[frm, slot], sib_recv.at[frm, slot], frm
+        )
+
+    half = rows // 2
+    beside = place + 1 - 2 * lax.rem(place, 2)
+    across = lax.rem(place + 2, group)
+    corner = group - 1 - place
+
+    def pass_on(part_of, frm, there):
+        at = x_all.at[core, frm, pl.ds(part_of * half, half)]
+        return to_seq(
+            at, at, diag_send.at[part_of], diag_recv.at[part_of], win * group + there
+        )
+
+    if square:
+        order = [beside, across, corner]
+        near_to(beside).start()
+        near_to(across).start()
+    else:
+        order = [lax.rem(place + k, group) for k in range(1, group)]
+        for there in order:
+            near_to(there).start()
     for k in range(1, n_trk):
-        sibling(k, x_ref, place).start()
-    x_all[core, place] = x_ref[...]
+        sibling(k, x_hbm, place).start()
+    own_copy = pltpu.make_async_copy(x_hbm, x_all.at[core, place], own_sem)
+    own_copy.start()
+    if head_hbm.shape[2] == tracks:
+        head_copy = pltpu.make_async_copy(head_hbm, head_ref, head_sem)
+    else:
+        at = pl.ds(pl.multiple_of(place * tracks, tracks), tracks)
+        head_copy = pltpu.make_async_copy(head_hbm.at[:, :, at], head_ref, head_sem)
+    head_copy.start()
 
     def tgt_copy(k):
         there = lax.rem(me + k, n_seq)
         return to_seq(tgt_ref.at[there], tgt_in.at[me], tgt_send.at[there], tgt_recv.at[me], there)
 
+    tgt_ref[...] = jnp.zeros_like(tgt_ref)
+    for w in range(windows):
+        for p in range(group):
+            tgt_ref[w * group + p, :capacity, :] = (
+                targets_ref[w, :, p * tracks:(p + 1) * tracks]
+            )
+
     @pl.loop(1, n_seq)
     def _(k):
         tgt_copy(k).start()
 
     tgt_in[me] = tgt_ref[me]
+
+    mem_ref[...] = jnp.zeros_like(mem_ref)
+    exons = starts_ref.shape[2]
+
+    @pl.loop(0, group)
+    def _(slot):
+        bins = (win * group + slot) * bin_dev + lax.broadcasted_iota(
+            jnp.int32, (genes, bin_dev), 1
+        )
+        for w in range(windows):
+            first, extent = starts_ref[w], lengths_ref[w]
+            count = jnp.zeros((genes, bin_dev), jnp.float32)
+            for e in range(exons):
+                begin = first[:, e:e + 1]
+                end = begin + extent[:, e:e + 1]
+                count += jnp.where((bins >= begin) & (bins < end), 1.0, 0.0)
+            mem_ref[slot, w * genes:(w + 1) * genes, w * bin_dev:(w + 1) * bin_dev] = (
+                count.astype(jnp.bfloat16)
+            )
+
+    owner_row = owner_ref[pl.ds(win, 1), :]
+    down = lax.broadcasted_iota(jnp.int32, (genes, genes), 0)
+    along = lax.broadcasted_iota(jnp.int32, (genes, genes), 1)
+    spread_row = jnp.broadcast_to(owner_row, (genes, genes))
+    owner_col = jnp.sum(jnp.where(down == along, spread_row, 0), axis=1, keepdims=True)
+    same = spread_row == owner_col
+    rank_col = jnp.sum(jnp.where(same & (along < down), 1, 0), axis=1, keepdims=True)
+    rank_row = jnp.sum(jnp.where(same & (down < along), 1, 0), axis=0, keepdims=True)
+    slot_col = owner_col * cap_pad + rank_col
+    slot_row = owner_row * cap_pad + rank_row
+    slots = n_seq * cap_pad
+    pick = jnp.where(
+        slot_col == lax.broadcasted_iota(jnp.int32, (genes, slots), 1), 1.0, 0.0
+    )
+    give = jnp.where(
+        slot_row == lax.broadcasted_iota(jnp.int32, (slots, genes), 0), 1.0, 0.0
+    )
 
     part[...] = jnp.zeros_like(part)
 
@@ -131,16 +187,37 @@
             mem_ref[slot], pred[...], preferred_element_type=jnp.float32
         ).reshape(part.shape)
 
-    for k in range(1, group + 1):
-        if k < group:
-            near_arrival(k).wait_recv()
-            frm = lax.rem(place + k, group)
-            for j in range(1, n_trk):
-                sibling(j, x_all.at[core, frm], frm).start()
-        slot = lax.rem(place + k - 1, group)
+    own_copy.wait()
+    head_copy.wait()
+
+    def hand_over(frm):
+        for j in range(1, n_trk):
+            sibling(j, x_all.at[core, frm], frm).start()
+
+    if square:
+        near_from(beside).wait_recv()
+        pass_on(0, beside, across).start()
+        hand_over(beside)
+        near_from(across).wait_recv()
+        pass_on(1, across, beside).start()
+        hand_over(across)
+        ready = [place, beside, across]
+    else:
+        ready = [place]
+    for slot in ready:
         for j in range(1, n_trk):
             sibling_arrival(j, slot).wait_recv()
         forward(slot)
+    for frm in order[len(ready) - 1:]:
+        if square:
+            pass_on(0, frm, across).wait_recv()
+            pass_on(1, frm, beside).wait_recv()
+        else:
+            near_from(frm).wait_recv()
+        hand_over(frm)
+        for j in range(1, n_trk):
+            sibling_arrival(j, frm).wait_recv()
+        forward(frm)
 
     def part_copy(k):
         there = lax.rem(win + k, windows)
@@ -160,7 +237,7 @@
         ).wait_recv()
 
     tgt = jnp.dot(
-        pick_ref[...], tgt_in[...].reshape(-1, tracks),
+        pick, tgt_in[...].reshape(-1, tracks),
         preferred_element_type=jnp.float32, precision=HIGHEST,
     )
     tsum = jnp.sum(tgt, axis=0, keepdims=True)
@@ -194,21 +271,21 @@
     loss = (-fit + tsum * log_total + 0.2 * (total - tsum * log_total)) / tsum
     loss_out[...] = jnp.broadcast_to(loss, loss_out.shape)
     gene_out[...] = jnp.dot(
-        give_ref[...], gene, preferred_element_type=jnp.float32, precision=HIGHEST
+        give, gene, preferred_element_type=jnp.float32, precision=HIGHEST
     ).reshape(gene_out.shape)
 
     def gene_copy(k):
         there = lax.rem(me + k, n_seq)
         return to_seq(
-            gene_out.at[there], gene_ref.at[me], gene_send.at[there], gene_recv.at[me], there
+            gene_out.at[there], gene_in.at[me], gene_send.at[there], gene_recv.at[me], there
         )
 
     def loss_copy(k):
         there = lax.rem(me + k, n_seq)
-        return to_seq(loss_out, loss_ref.at[me], loss_send.at[there], loss_recv.at[me], there)
-
-    gene_ref[me] = gene_out[me]
-    loss_ref[me] = loss_out[...]
+        return to_seq(loss_out, loss_in.at[me], loss_send.at[there], loss_recv.at[me], there)
+
+    gene_in[me] = gene_out[me]
+    loss_in[me] = loss_out[...]
 
     for k in range(1, windows):
         frm = lax.rem(win + k, windows)
@@ -237,7 +314,8 @@
             block_out.at[there], block_in.at[me], block_send.at[there], block_recv.at[me], there
         )
 
-    for c in range(n_trk):
+    for i in range(n_trk):
+        c = lax.rem(2 * n_trk - 1 - win * n_trk // windows + i, n_trk)
         acc[...] = jnp.zeros_like(acc)
 
         @pl.loop(0, group)
@@ -272,15 +350,15 @@
         whole = block_in[p].astype(jnp.float32)
         for w in range(1, windows):
             whole += block_in[w * group + p].astype(jnp.float32)
-        grad_ref[p] = whole
+        grad_ref[:, p * tracks:(p + 1) * tracks] = whole[:own_rows]
 
     @pl.loop(1, n_seq)
     def _(k):
         frm = lax.rem(me + k, n_seq)
         to_seq(
-            gene_out.at[frm], gene_ref.at[frm], gene_send.at[frm], gene_recv.at[frm], frm
+            gene_out.at[frm], gene_in.at[frm], gene_send.at[frm], gene_recv.at[frm], frm
         ).wait_recv()
-        to_seq(loss_out, loss_ref.at[frm], loss_send.at[frm], loss_recv.at[frm], frm).wait_recv()
+        to_seq(loss_out, loss_in.at[frm], loss_send.at[frm], loss_recv.at[frm], frm).wait_recv()
         tgt_copy(k).wait_send()
         gene_copy(k).wait_send()
         loss_copy(k).wait_send()
@@ -289,12 +367,23 @@
     for k in range(1, windows):
         part_copy(k).wait_send()
         grads_copy(k).wait_send()
-    for k in range(1, group):
-        near(k).wait_send()
+    for w in range(windows):
+        for p in range(group):
+            at = slice(p * tracks, (p + 1) * tracks)
+            gene_ref[w, :, at] = gene_in[w * group + p, :capacity, :]
+            loss_ref[w:w + 1, at] = loss_in[w * group + p, :1, :]
+
+    if square:
+        near_to(beside).wait_send()
+        near_to(across).wait_send()
+        pass_on(0, beside, across).wait_send()
+        pass_on(1, across, beside).wait_send()
+    else:
+        for there in order:
+            near_to(there).wait_send()
     for k in range(1, n_trk):
-        sibling(k, x_ref, place).wait_send()
-        for j in range(1, group):
-            frm = lax.rem(place + j, group)
+        sibling(k, x_hbm, place).wait_send()
+        for frm in order:
             sibling(k, x_all.at[core, frm], frm).wait_send()
 
 
@@ -310,7 +399,6 @@
     genes = gene_owner.shape[1]
     capacity = gene_targets.shape[1]
     group = n_seq // windows
-    win, place = me // group, me % group
     depth, track_dev = head.shape
     tracks = track_dev // group
     rows = windows * bin_dev
@@ -319,37 +407,29 @@
     cap_pad = round_up(capacity, 8)
     bf16, f32 = jnp.bfloat16, jnp.float32
 
-    positions = win * group * bin_dev + jnp.arange(group * bin_dev, dtype=jnp.int32)
-    cover = coverage(exon_starts, exon_lengths, positions).reshape(windows, genes, group, bin_dev)
-    same = jnp.eye(windows, dtype=f32)
-    mem = cover.transpose(2, 0, 1, 3)[:, :, :, None, :] * same[None, :, None, :, None]
-    mem = mem.reshape(group, windows * genes, rows).astype(bf16)
-    slot_here = lax.dynamic_index_in_dim(slot_table(gene_owner, capacity), win, 0, keepdims=False)
-    padded = slot_here // capacity * cap_pad + slot_here % capacity
-    every = jnp.arange(n_seq * cap_pad, dtype=jnp.int32)
-    pick = (padded[:, None] == every[None, :]).astype(f32)
-    give = (padded[None, :] == every[:, None]).astype(f32)
-    head_here = lax.dynamic_slice_in_dim(head, place * tracks, tracks, 1).reshape(
-        n_trk, chans, tracks
-    )
-    tgt = gene_targets.reshape(windows, capacity, group, tracks).transpose(0, 2, 1, 3)
-    tgt = jnp.pad(
-        tgt.reshape(n_seq, capacity, tracks), ((0, 0), (0, cap_pad - capacity), (0, 0))
-    )
+    head_parts = head.reshape(n_trk, chans, track_dev)
+    if tracks % 128:
+        head_parts = lax.dynamic_slice_in_dim(head_parts, me % group * tracks, tracks, 2)
 
     dma = pltpu.SemaphoreType.DMA
     vmem = pl.BlockSpec(memory_space=pltpu.VMEM)
+    hbm = pl.BlockSpec(memory_space=pl.ANY)
     grad, gene, loss = pl.pallas_call(
         functools.partial(kernel, (n_seq, n_trk, windows, group, genes, own_rows)),
         out_shape=(
-            jax.ShapeDtypeStruct((group, row_pad, tracks), f32),
-            jax.ShapeDtypeStruct((n_seq, cap_pad, tracks), f32),
-            jax.ShapeDtypeStruct((n_seq, 8, tracks), f32),
+            jax.ShapeDtypeStruct((own_rows, track_dev), f32),
+            jax.ShapeDtypeStruct((windows, capacity, track_dev), f32),
+            jax.ShapeDtypeStruct((windows, track_dev), f32),
         ),
-        in_specs=[vmem] * 6,
+        in_specs=[hbm, hbm, vmem, vmem, vmem, vmem],
         out_specs=(vmem, vmem, vmem),
         scratch_shapes=[
             pltpu.VMEM((n_trk, group, rows, chans), bf16),
+            pltpu.VMEM((n_trk, chans, tracks), bf16),
+            pltpu.VMEM((group, windows * genes, rows), bf16),
+            pltpu.VMEM((n_seq, cap_pad, tracks), f32),
+            pltpu.VMEM((n_seq, cap_pad, tracks), f32),
+            pltpu.VMEM((n_seq, 8, tracks), f32),
             pltpu.VMEM((rows, tracks), bf16),
             pltpu.VMEM((group, rows, tracks), f32),
             pltpu.VMEM((windows, genes, tracks), f32),
@@ -370,16 +450,17 @@
             dma((n_seq,)), dma((n_seq,)),
             dma((n_seq,)), dma((n_seq,)),
             dma((n_seq,)), dma((n_seq,)),
+            dma((2,)), dma((2,)), dma, dma,
         ],
         compiler_params=pltpu.CompilerParams(
             collective_id=0, has_side_effects=True, vmem_limit_bytes=60 * 1024 * 1024
         ),
-    )(embeddings.reshape(rows, chans), head_here, mem, pick, give, tgt)
-
-    grad_head = grad[:, :own_rows].transpose(1, 0, 2).reshape(own_rows, track_dev)
-    gene_here = gene[:, :capacity].reshape(windows, group, capacity, tracks)
-    gene_here = gene_here.transpose(0, 2, 1, 3).reshape(windows, capacity, track_dev)
-    return gene_here, loss[:, 0].reshape(windows, track_dev), grad_head
+    )(
+        embeddings.reshape(rows, chans), head_parts, exon_starts, exon_lengths, gene_owner,
+        gene_targets,
+    )
+
+    return gene, loss, grad
 
 
 def solution(mesh):

time: 158 us -> 138 us (0.87)
  the two profiles are of different devices: /device:TPU:14 before, /device:TPU:31 now
where the time goes in v2:
time: 138 us; the launch traced here: 137 us
  Pallas kernels  126 us (91%)
  local copies, waits for them, and re-layouts  10.3 us (7%)
    pallas_call x1, Pallas kernels, per_device(): pl.pallas_call(functools.partial(kernel, (n_seq, n_trk, windows, group, g...  126 us
    unnamed x6, local copies, waits for them, and re-layouts  10.3 us

profile of v2, /device:TPU:31, one launch (start us, length us, event | category | flops | bytes accessed | tf_op | source)
XLA Modules:
  0.0 137.3 jit_solution(3657054724932095790)
XLA Ops:
  0.6 1.4 %copy.10.starts_ref = s32[4,32,8]{2,1,0:T(8,128)} copy(s32[4,32,8]{1,2,0:T(8,128)} %param.8) | data formatting | bytes 8192 | tf_op args[2]
  2.1 1.4 %copy.11.lengths_ref = s32[4,32,8]{2,1,0:T(8,128)} copy(s32[4,32,8]{1,2,0:T(8,128)} %param.9) | data formatting | bytes 8192 | tf_op args[3]
  3.5 2.3 %copy.9 = bf16[4,128,960]{2,1,0:T(8,128)(2,1)} copy(bf16[4,128,960]{1,2,0:T(8,128)(2,1)} %param.6) | data formatting | bytes 1966080 | tf_op args[0]
  5.8 126.4 %shard_map.85 = (f32[120,2048]{1,0:T(8,128)}, f32[4,4,2048]{2,1,0:T(4,128)}, f32[4,2048]{1,0:T(4,128)}) custom-call(bf16[512,960]{1,0:T(8,128)(2,1)} %bitcast.3, bf16[2,960,2048]{2,1,0:T(8,128)(2,1)} %bitcast.2, s32[4,32,8]{2,1,0:T(8,128)} %copy.10.starts_ref, s32[4,32,8]{2,1,0:T(8,128)} %copy.11.lengths_ref, s32[4,32]{1,0:T(4,128)} %owner_ref.1, ...), custom_call_target="tpu_custom_call" | custom-call | tf_op jit(solution)/shard_map/pallas_call | solution.py:417
  132.2 1.6 %copy.15 = f32[4,4,2048]{2,1,0:T(4,128)} copy(f32[4,4,2048]{2,1,0:T(4,128)} %get-tuple-element.12) | data formatting | bytes 262144
  133.7 1.4 %copy.16 = f32[4,2048]{1,0:T(4,128)} copy(f32[4,2048]{1,0:T(4,128)} %get-tuple-element.13) | data formatting | bytes 65536
  135.1 2.2 %copy.17 = f32[120,2048]{1,0:T(8,128)} copy(f32[120,2048]{1,0:T(8,128)} %get-tuple-element.14) | data formatting | bytes 1966080

commit v3 on v2

--- a/solution.py
+++ b/solution.py
@@ -13,12 +13,12 @@
 
 def kernel(
     dims,
-    x_hbm, head_hbm, starts_ref, lengths_ref, owner_ref, targets_ref,
+    x_hbm, head_hbm, exons_ref, owner_ref, targets_ref,
     grad_ref, gene_ref, loss_ref,
     x_all, head_ref, mem_ref, tgt_ref, gene_in, loss_in, pred, sig, part, part_in, grads, tgt_in, gene_out, loss_out, lgrad, acc, block_out, block_in,
     near_send, near_recv, sib_send, sib_recv, tgt_send, tgt_recv, part_send, part_recv,
     grads_send, grads_recv, gene_send, gene_recv, loss_send, loss_recv, block_send, block_recv,
-    diag_send, diag_recv, own_sem, head_sem,
+    diag_send, diag_recv, own_sem, head_sem, pair_in, pair_send, pair_recv,
 ):
     n_seq, n_trk, windows, group, genes, own_rows = dims
     me = lax.axis_index("seq")
@@ -130,7 +130,7 @@
     tgt_in[me] = tgt_ref[me]
 
     mem_ref[...] = jnp.zeros_like(mem_ref)
-    exons = starts_ref.shape[2]
+    exons = exons_ref.shape[2] // 2
 
     @pl.loop(0, group)
     def _(slot):
@@ -138,11 +138,11 @@
             jnp.int32, (genes, bin_dev), 1
         )
         for w in range(windows):
-            first, extent = starts_ref[w], lengths_ref[w]
+            table = exons_ref[w]
             count = jnp.zeros((genes, bin_dev), jnp.float32)
             for e in range(exons):
-                begin = first[:, e:e + 1]
-                end = begin + extent[:, e:e + 1]
+                begin = table[:, e:e + 1]
+                end = begin + table[:, exons + e:exons + e + 1]
                 count += jnp.where((bins >= begin) & (bins < end), 1.0, 0.0)
             mem_ref[slot, w * genes:(w + 1) * genes, w * bin_dev:(w + 1) * bin_dev] = (
                 count.astype(jnp.bfloat16)
@@ -314,6 +314,16 @@
             block_out.at[there], block_in.at[me], block_send.at[there], block_recv.at[me], there
         )
 
+    paired = windows == 4 and n_trk == 2
+    partner = win + 1 - 2 * lax.rem(win, 2)
+    opposite = lax.rem(win + 2, windows)
+
+    def pair_copy():
+        at = pl.ds(lax.rem(partner + 2, windows) * group, group)
+        return to_seq(
+            block_out.at[at], pair_in, pair_send, pair_recv, partner * group + place
+        )
+
     for i in range(n_trk):
         c = lax.rem(2 * n_trk - 1 - win * n_trk // windows + i, n_trk)
         acc[...] = jnp.zeros_like(acc)
@@ -333,24 +343,51 @@
                 value = jnp.concatenate([value, jnp.zeros((spare, tracks), jnp.bfloat16)], axis=0)
             block_out[there] = value
 
-            @pl.when(me != there)
-            def _():
-                block_copy(there).start()
+            if i > 0 or not paired:
+                @pl.when(me != there)
+                def _():
+                    block_copy(there).start()
+
+        if i == 0 and paired:
+            pair_copy().start()
 
     block_in[me] = block_out[me]
-
-    @pl.loop(1, n_seq)
-    def _(k):
-        frm = lax.rem(me + k, n_seq)
-        to_seq(
+    if paired:
+        pair_copy().wait_recv()
+        for p in range(group):
+            there = opposite * group + p
+            block_out[there] = (
+                block_out[there].astype(jnp.float32) + pair_in[p].astype(jnp.float32)
+            ).astype(jnp.bfloat16)
+            block_copy(there).start()
+        terms = [win, partner, opposite]
+    else:
+        terms = [lax.rem(win + k, windows) for k in range(windows)]
+
+    def block_arrival(frm):
+        return to_seq(
             block_out.at[frm], block_in.at[frm], block_send.at[frm], block_recv.at[frm], frm
-        ).wait_recv()
+        )
+
+    for k in range(1, group):
+        block_arrival(win * group + lax.rem(place + k, group)).wait_recv()
+    for w in terms[1:]:
+        for p in range(group):
+            block_arrival(w * group + p).wait_recv()
 
     for p in range(group):
-        whole = block_in[p].astype(jnp.float32)
-        for w in range(1, windows):
+        whole = block_in[terms[0] * group + p].astype(jnp.float32)
+        for w in terms[1:]:
             whole += block_in[w * group + p].astype(jnp.float32)
         grad_ref[:, p * tracks:(p + 1) * tracks] = whole[:own_rows]
+
+    for k in range(1, group):
+        block_copy(win * group + lax.rem(place + k, group)).wait_send()
+    for w in terms[1:]:
+        for p in range(group):
+            block_copy(w * group + p).wait_send()
+    if paired:
+        pair_copy().wait_send()
 
     @pl.loop(1, n_seq)
     def _(k):
@@ -362,7 +399,6 @@
         tgt_copy(k).wait_send()
         gene_copy(k).wait_send()
         loss_copy(k).wait_send()
-        block_copy(frm).wait_send()
 
     for k in range(1, windows):
         part_copy(k).wait_send()
@@ -421,7 +457,7 @@
             jax.ShapeDtypeStruct((windows, capacity, track_dev), f32),
             jax.ShapeDtypeStruct((windows, track_dev), f32),
         ),
-        in_specs=[hbm, hbm, vmem, vmem, vmem, vmem],
+        in_specs=[hbm, hbm, vmem, vmem, vmem],
         out_specs=(vmem, vmem, vmem),
         scratch_shapes=[
             pltpu.VMEM((n_trk, group, rows, chans), bf16),
@@ -451,13 +487,14 @@
             dma((n_seq,)), dma((n_seq,)),
             dma((n_seq,)), dma((n_seq,)),
             dma((2,)), dma((2,)), dma, dma,
+            pltpu.VMEM((group, row_pad, tracks), bf16), dma, dma,
         ],
         compiler_params=pltpu.CompilerParams(
             collective_id=0, has_side_effects=True, vmem_limit_bytes=60 * 1024 * 1024
         ),
     )(
-        embeddings.reshape(rows, chans), head_parts, exon_starts, exon_lengths, gene_owner,
-        gene_targets,
+        embeddings.reshape(rows, chans), head_parts,
+        jnp.concatenate([exon_starts, exon_lengths], axis=2), gene_owner, gene_targets,
     )
 
     return gene, loss, grad

time: 138 us -> 121 us (0.88)
  the two profiles are of different devices: /device:TPU:31 before, /device:TPU:14 now
where the time goes in v3:
time: 121 us; the launch traced here: 118 us
  Pallas kernels  108 us (89%)
  local copies, waits for them, and re-layouts  9.04 us (7%)
    pallas_call x1, Pallas kernels, per_device(): pl.pallas_call(functools.partial(kernel, (n_seq, n_trk, windows, group, g...  108 us
    unnamed x6, local copies, waits for them, and re-layouts  9.04 us

profile of v3, /device:TPU:14, one launch (start us, length us, event | category | flops | bytes accessed | tf_op | source)
XLA Modules:
  0.0 118.3 jit_solution(7834392231577086517)
XLA Ops:
  0.6 0.8 copy.10
  1.4 0.8 copy.11
  2.2 0.7 pad_add_fusion.exons_ref
  3.0 2.3 %copy.9 = bf16[4,128,960]{2,1,0:T(8,128)(2,1)} copy(bf16[4,128,960]{1,2,0:T(8,128)(2,1)} %param.6) | data formatting | bytes 1966080 | tf_op args[0]
  5.2 107.9 %shard_map.85 = (f32[120,2048]{1,0:T(8,128)}, f32[4,4,2048]{2,1,0:T(4,128)}, f32[4,2048]{1,0:T(4,128)}) custom-call(bf16[512,960]{1,0:T(8,128)(2,1)} %bitcast.3, bf16[2,960,2048]{2,1,0:T(8,128)(2,1)} %bitcast.2, s32[4,32,16]{2,1,0:T(8,128)} %pad_add_fusion.exons_ref, s32[4,32]{1,0:T(4,128)} %owner_ref.1, f32[4,4,2048]{2,1,0:T(4,128)} %targets_ref.1), custom_call_target="tpu_custom_call" | custom-call | tf_op jit(solution)/shard_map/pallas_call | solution.py:453
  113.1 1.6 %copy.15 = f32[4,4,2048]{2,1,0:T(4,128)} copy(f32[4,4,2048]{2,1,0:T(4,128)} %get-tuple-element.12) | data formatting | bytes 262144
  114.7 1.4 %copy.16 = f32[4,2048]{1,0:T(4,128)} copy(f32[4,2048]{1,0:T(4,128)} %get-tuple-element.13) | data formatting | bytes 65536
  116.0 2.2 %copy.17 = f32[120,2048]{1,0:T(8,128)} copy(f32[120,2048]{1,0:T(8,128)} %get-tuple-element.14) | data formatting | bytes 1966080

commit v4 on v3

--- a/solution.py
+++ b/solution.py
@@ -318,10 +318,11 @@
     partner = win + 1 - 2 * lax.rem(win, 2)
     opposite = lax.rem(win + 2, windows)
 
-    def pair_copy():
-        at = pl.ds(lax.rem(partner + 2, windows) * group, group)
-        return to_seq(
-            block_out.at[at], pair_in, pair_send, pair_recv, partner * group + place
+    def pair_copy(p):
+        there = lax.rem(partner + 2, windows) * group + p
+        return to_seq(
+            block_out.at[there], pair_in.at[p], pair_send.at[p], pair_recv.at[p],
+            partner * group + place,
         )
 
     for i in range(n_trk):
@@ -349,12 +350,13 @@
                     block_copy(there).start()
 
         if i == 0 and paired:
-            pair_copy().start()
+            for p in range(group):
+                pair_copy(p).start()
 
     block_in[me] = block_out[me]
     if paired:
-        pair_copy().wait_recv()
         for p in range(group):
+            pair_copy(p).wait_recv()
             there = opposite * group + p
             block_out[there] = (
                 block_out[there].astype(jnp.float32) + pair_in[p].astype(jnp.float32)
@@ -387,7 +389,8 @@
         for p in range(group):
             block_copy(w * group + p).wait_send()
     if paired:
-        pair_copy().wait_send()
+        for p in range(group):
+            pair_copy(p).wait_send()
 
     @pl.loop(1, n_seq)
     def _(k):
@@ -487,7 +490,7 @@
             dma((n_seq,)), dma((n_seq,)),
             dma((n_seq,)), dma((n_seq,)),
             dma((2,)), dma((2,)), dma, dma,
-            pltpu.VMEM((group, row_pad, tracks), bf16), dma, dma,
+            pltpu.VMEM((group, row_pad, tracks), bf16), dma((group,)), dma((group,)),
         ],
         compiler_params=pltpu.CompilerParams(
             collective_id=0, has_side_effects=True, vmem_limit_bytes=60 * 1024 * 1024

time: 121 us -> 120 us (level); the launches traced: 118 us -> 119 us
  no operation moved by 1% of the time
where the time goes in v4:
time: 120 us; the launch traced here: 119 us
  Pallas kernels  109 us (91%)
  local copies, waits for them, and re-layouts  9.04 us (8%)
    pallas_call x1, Pallas kernels, per_device(): pl.pallas_call(functools.partial(kernel, (n_seq, n_trk, windows, group, g...  109 us
    unnamed x6, local copies, waits for them, and re-layouts  9.04 us

profile of v4, /device:TPU:14, one launch (start us, length us, event | category | flops | bytes accessed | tf_op | source)
XLA Modules:
  0.0 119.0 jit_solution(13870764529603485460)
XLA Ops:
  0.6 0.8 copy.10
  1.4 0.8 copy.11
  2.2 0.7 pad_add_fusion.exons_ref
  3.0 2.3 %copy.9 = bf16[4,128,960]{2,1,0:T(8,128)(2,1)} copy(bf16[4,128,960]{1,2,0:T(8,128)(2,1)} %param.6) | data formatting | bytes 1966080 | tf_op args[0]
  5.2 108.6 %shard_map.85 = (f32[120,2048]{1,0:T(8,128)}, f32[4,4,2048]{2,1,0:T(4,128)}, f32[4,2048]{1,0:T(4,128)}) custom-call(bf16[512,960]{1,0:T(8,128)(2,1)} %bitcast.3, bf16[2,960,2048]{2,1,0:T(8,128)(2,1)} %bitcast.2, s32[4,32,16]{2,1,0:T(8,128)} %pad_add_fusion.exons_ref, s32[4,32]{1,0:T(4,128)} %owner_ref.1, f32[4,4,2048]{2,1,0:T(4,128)} %targets_ref.1), custom_call_target="tpu_custom_call" | custom-call | tf_op jit(solution)/shard_map/pallas_call | solution.py:456
  113.9 1.6 %copy.15 = f32[4,4,2048]{2,1,0:T(4,128)} copy(f32[4,4,2048]{2,1,0:T(4,128)} %get-tuple-element.12) | data formatting | bytes 262144
  115.4 1.4 %copy.16 = f32[4,2048]{1,0:T(4,128)} copy(f32[4,2048]{1,0:T(4,128)} %get-tuple-element.13) | data formatting | bytes 65536
  116.8 2.2 %copy.17 = f32[120,2048]{1,0:T(8,128)} copy(f32[120,2048]{1,0:T(8,128)} %get-tuple-element.14) | data formatting | bytes 1966080
